TPU v7x, 128 devices: a whole 4x4x4 slice. The times are simulated.
128 devices in a mesh: grp: 4 (over x), mem: 32 (over y, z, core).
Axes of the slice: x: 4, y: 4, z: 4, core: 2. Of those that a mesh axis runs over, the one named last changes fastest.
Arguments:
- prior_trajectory: bfloat16 [128, 1024, 8, 512], P('mem', 'grp'), may hold values from -6 to 6
- measured_equivalent: bfloat16 [128, 1024, 1024], P('mem', 'grp'), may hold values from -6 to 6
- measured_datum: float32 [1024, 1024], P(('grp', 'mem')), may hold values from -10 to 10
- weighted_inverse_noise: bfloat16 [1024, 1024], P(('grp', 'mem')), may hold values from 0.049804688 to 1
- local_tallies: int32 [1024], P(('grp', 'mem')), may hold values from 1 to 1024, as said below
- device_assignment: int32 [1024], P(('grp', 'mem')), may hold values from 0 to 3, as said below
Outputs:
- analysis: bfloat16 [128, 1024, 8, 512], P(None, ('grp', 'mem'))
- slot_weights: bfloat16 [1024, 128, 128], P(('grp', 'mem'))
Inputs may be any that keep to these rules, and one draw needn't show every extreme that they name: `local_tallies`: at least one block of every draw has exactly 1024 local observations. `device_assignment`: among the 32 blocks with one m (see the steps), each value is named by exactly 8 blocks; among the 8 blocks of one device, no value is named by more than 4 blocks, and every device reaches that bound.
All inputs are finite; a program needn't handle non-finite values.
Results may differ from a plain program's by a relative error of at most 0.012.
Values may be sent and summed in bfloat16 or wider, within the bound.
A program may use at most 128 MiB of HBM per device.

v0:
```python
import functools
import math

import jax
import jax.numpy as jnp
from jax import lax
from jax.experimental import pallas as pl
from jax.experimental.pallas import tpu as pltpu
from jax.sharding import PartitionSpec as P

ITERS = 12
MEM = 128
NBLK = 8
COLS = 8
VERT = 512
OBS = 1024
NGRP = 4
NMEM = 32
OWN = MEM // NMEM
CAP = NBLK // 2
ROWS = MEM * COLS
MESH = pl.DeviceIdType.MESH
HIGH = lax.Precision.HIGHEST
F32 = jnp.float32
BF16 = jnp.bfloat16


def mm(a, b):
    return jnp.dot(a, b, precision=HIGH, preferred_element_type=F32)


def analysis_kernel(
    prior, equiv, datum, winv, tally, table,
    out, slots,
    xg, yg, yf, kron, spread, ymat, zmat, pmat, scales, wts, pack, got, tabs, tab_mine,
    x_send, x_recv, y_send, y_recv, g_send, g_recv, t_send, t_recv, x_loc, y_loc,
):
    g = lax.axis_index("grp")
    m = lax.axis_index("mem")
    row, col, core = m // 8, (m // 2) % 4, m % 2

    def peer(i):
        return (((row + i // 8) % 4) * 4 + (col + (i // 2) % 4) % 4) * 2 + (core + i % 2) % 2

    barrier = pltpu.get_barrier_semaphore()

    def greet(i, carry):
        pl.semaphore_signal(barrier, inc=1, device_id=(g, peer(i)), device_id_type=MESH)
        return carry

    lax.fori_loop(1, NMEM, greet, 0)
    for d in range(1, NGRP):
        pl.semaphore_signal(barrier, inc=1, device_id=((g + d) % NGRP, m), device_id_type=MESH)
    pl.semaphore_wait(barrier, NMEM - 1 + NGRP - 1)

    def send_obs(i, carry):
        p = peer((i * 11) % NMEM)
        pltpu.make_async_remote_copy(
            src_ref=equiv.at[:, p], dst_ref=yg.at[pl.ds(OWN * m, OWN)],
            send_sem=y_send, recv_sem=y_recv, device_id=(g, p), device_id_type=MESH,
        ).start()
        return carry

    lax.fori_loop(1, NMEM, send_obs, 0)
    own_y = pltpu.make_async_copy(equiv.at[:, m], yg.at[pl.ds(OWN * m, OWN)], y_loc)
    own_y.start()

    def send_block(q, carry):
        def send_prior(i, inner):
            p = peer((i * 11) % NMEM)
            pltpu.make_async_remote_copy(
                src_ref=prior.at[:, pl.ds(NBLK * p + q, 1)],
                dst_ref=xg.at[pl.ds(OWN * m, OWN), pl.ds(q, 1)],
                send_sem=x_send, recv_sem=x_recv.at[q], device_id=(g, p), device_id_type=MESH,
            ).start()
            return inner

        return lax.fori_loop(1, NMEM, send_prior, carry)

    lax.fori_loop(0, NBLK, send_block, 0)
    own_x = pltpu.make_async_copy(
        prior.at[:, pl.ds(NBLK * m, NBLK)], xg.at[pl.ds(OWN * m, OWN)], x_loc)
    own_x.start()

    for j in range(NBLK):
        tab_mine[j:j + 1, :] = jnp.full((1, 128), table[j], jnp.int32)
    tab_copies = []
    for d in range(1, NGRP):
        c = pltpu.make_async_remote_copy(
            src_ref=tab_mine, dst_ref=tabs.at[g],
            send_sem=t_send.at[d], recv_sem=t_recv.at[d],
            device_id=((g + d) % NGRP, m), device_id_type=MESH)
        c.start()
        tab_copies.append(c)

    spread[...] = (
        lax.broadcasted_iota(jnp.int32, (MEM, ROWS), 0)
        == lax.broadcasted_iota(jnp.int32, (MEM, ROWS), 1) // COLS
    ).astype(F32).astype(BF16)
    eye = (
        lax.broadcasted_iota(jnp.int32, (MEM, MEM), 0)
        == lax.broadcasted_iota(jnp.int32, (MEM, MEM), 1)
    ).astype(F32)

    own_y.wait()
    landed = yg.at[pl.ds(0, MEM - OWN)]
    pltpu.make_async_copy(landed, landed, y_recv).wait()

    def add_member(k, acc):
        return acc + yg[k].astype(F32)

    total = lax.fori_loop(0, MEM, add_member, jnp.zeros((NBLK, OBS), F32))
    ybar = total * (1.0 / MEM)
    yf_mean = ybar

    def take_mean(k, carry):
        d = (yg[k].astype(F32) - yf_mean).astype(BF16).astype(F32)
        for ch in range(OBS // 128):
            yf[ch, pl.ds(pl.multiple_of(k * NBLK, NBLK), NBLK), :] = d[:, ch * 128:(ch + 1) * 128]
        return carry

    lax.fori_loop(0, MEM, take_mean, 0)
    innov = (datum[...] - ybar).astype(BF16).astype(F32)
    rinv = winv[...].astype(F32)
    for b in range(NBLK):
        live = lax.broadcasted_iota(jnp.int32, (1, OBS), 1) < tally[b]
        rmask = jnp.where(live, rinv[b:b + 1, :], 0.0)
        yp = jnp.concatenate(
            [yf[ch, pl.ds(b, MEM, stride=NBLK), :] for ch in range(OBS // 128)], axis=1)
        yr = (yp * rmask).astype(BF16)
        both = jnp.concatenate(
            [yp.astype(BF16), jnp.broadcast_to(innov[b:b + 1, :], (MEM, OBS)).astype(BF16)], axis=0)
        prod = lax.dot_general(yr, both, (((1,), (1,)), ((), ())), preferred_element_type=F32)
        amat = (MEM - 1.0) * eye + prod[:, :MEM]
        pmat[b] = prod[:, MEM:]
        scale = jnp.sqrt(jnp.sum(jnp.sum(amat * amat, axis=1, keepdims=True), axis=0, keepdims=True))
        scales[b] = jnp.broadcast_to(scale, (8, 128))
        ymat[b] = amat / scale
        zmat[b] = eye

    def newton(it, carry):
        ts = [1.5 * eye - 0.5 * mm(zmat[b], ymat[b]) for b in range(NBLK)]
        for b in range(NBLK):
            ymat[b] = mm(ymat[b], ts[b])
            zmat[b] = mm(ts[b], zmat[b])
        return carry

    lax.fori_loop(0, ITERS, newton, 0)

    for b in range(NBLK):
        root = zmat[b] / jnp.sqrt(scales[b][:1])
        wmean = mm(root, mm(root, pmat[b]))
        full = math.sqrt(MEM - 1.0) * root + wmean
        full = full + (1.0 - jnp.sum(full, axis=0, keepdims=True)) / MEM
        wts[b] = full.astype(BF16)

    within = []
    for j in range(NBLK):
        n = jnp.int32(0)
        for k in range(j):
            n = n + (table[k] == table[j]).astype(jnp.int32)
        within.append(n)
    for t in range(NGRP):
        for w in range(CAP):
            src = jnp.int32(0)
            for j in range(NBLK):
                src = src + jnp.int32(j) * ((table[j] == t) & (within[j] == w)).astype(jnp.int32)
            pack[t, w] = wts[src]
    w_copies = []
    for d in range(1, NGRP):
        to = (g + d) % NGRP
        c = pltpu.make_async_remote_copy(
            src_ref=pack.at[to], dst_ref=got.at[g],
            send_sem=g_send.at[d], recv_sem=g_recv.at[d],
            device_id=(to, m), device_id_type=MESH)
        c.start()
        w_copies.append(c)

    mask = (
        lax.broadcasted_iota(jnp.int32, (COLS, ROWS), 0)
        == lax.broadcasted_iota(jnp.int32, (COLS, ROWS), 1) % COLS
    ).astype(F32)

    def expand(b, carry):
        wide = lax.dot_general(
            wts[b], spread[...], (((0,), (0,)), ((), ())), preferred_element_type=F32)
        kron[b] = (wide[:, None, :] * mask[None]).reshape(ROWS, ROWS).astype(BF16)
        return carry

    lax.fori_loop(0, NBLK, expand, 0)

    for c in tab_copies:
        c.wait()
    for c in w_copies:
        c.wait()
    tabs[g] = tab_mine[...]
    got[g] = pack[g]
    base = jnp.zeros((1, 128), jnp.int32)
    ranks = []
    for gg in range(NGRP):
        hits = tabs[gg] == g
        count = jnp.sum(hits.astype(F32), axis=0, keepdims=True).astype(jnp.int32)
        for w in range(CAP):
            ranks.append(jnp.where(count > w, base + w, -1))
        base = base + count
    for k in range(NBLK):
        acc = jnp.zeros((MEM, MEM), F32)
        for gg in range(NGRP):
            for w in range(CAP):
                acc = jnp.where(ranks[gg * CAP + w] == k, got[gg, w].astype(F32), acc)
        slots[k] = acc.astype(BF16)

    own_x.wait()
    step = MEM // 4

    def mix(q, carry):
        here = xg.at[pl.ds(0, MEM - OWN), pl.ds(q, 1)]
        pltpu.make_async_copy(here, here, x_recv.at[q]).wait()
        state = xg[:, q].astype(F32).reshape(ROWS, VERT).astype(BF16)
        for part in range(4):
            mixed = jnp.dot(
                kron[q, part * step * COLS:(part + 1) * step * COLS, :], state,
                preferred_element_type=F32)
            out[part * step:(part + 1) * step, q] = mixed.reshape(step, COLS, VERT).astype(BF16)
        return carry

    lax.fori_loop(0, NBLK, mix, 0)

    sent = yg.at[pl.ds(0, MEM - OWN)]
    pltpu.make_async_copy(sent, sent, y_send).wait()
    sent = xg.at[pl.ds(0, MEM - OWN)]
    pltpu.make_async_copy(sent, sent, x_send).wait()


def store_kernel(analysis, slots, out, out_slots, sems):
    part = MEM // 8
    copies = [
        pltpu.make_async_copy(analysis.at[pl.ds(k * part, part)], out.at[pl.ds(k * part, part)], sems.at[k])
        for k in range(8)
    ]
    copies.append(pltpu.make_async_copy(slots, out_slots, sems.at[8]))
    for c in copies:
        c.start()
    for c in copies:
        c.wait()


def body(prior, equiv, datum, winv, tally, table):
    vmem = pl.BlockSpec(memory_space=pltpu.VMEM)
    smem = pl.BlockSpec(memory_space=pltpu.SMEM)
    hbm = pl.BlockSpec(memory_space=pltpu.HBM)
    dma = pltpu.SemaphoreType.DMA
    equiv = equiv.reshape(OWN, NMEM, NBLK, OBS)
    analysis, slots = pl.pallas_call(
        analysis_kernel,
        out_shape=(
            pltpu.VMEM((MEM, NBLK, COLS, VERT), BF16),
            pltpu.VMEM((NBLK, MEM, MEM), BF16),
        ),
        in_specs=[hbm, hbm, vmem, vmem, smem, smem],
        out_specs=(vmem, vmem),
        scratch_shapes=[
            pltpu.VMEM((MEM, NBLK, COLS, VERT), BF16),
            pltpu.VMEM((MEM, NBLK, OBS), BF16),
            pltpu.VMEM((OBS // 128, MEM * NBLK, 128), F32),
            pltpu.VMEM((NBLK, ROWS, ROWS), BF16),
            pltpu.VMEM((MEM, ROWS), BF16),
            pltpu.VMEM((NBLK, MEM, MEM), F32),
            pltpu.VMEM((NBLK, MEM, MEM), F32),
            pltpu.VMEM((NBLK, MEM, MEM), F32),
            pltpu.VMEM((NBLK, 8, 128), F32),
            pltpu.VMEM((NBLK, MEM, MEM), BF16),
            pltpu.VMEM((NGRP, CAP, MEM, MEM), BF16),
            pltpu.VMEM((NGRP, CAP, MEM, MEM), BF16),
            pltpu.VMEM((NGRP, NBLK, 128), jnp.int32),
            pltpu.VMEM((NBLK, 128), jnp.int32),
            dma, dma((NBLK,)), dma, dma,
            dma((NGRP,)), dma((NGRP,)), dma((NGRP,)), dma((NGRP,)), dma, dma,
        ],
        compiler_params=pltpu.CompilerParams(
            collective_id=0, has_side_effects=True, vmem_limit_bytes=50 << 20),
        name="analyse",
    )(prior, equiv, datum, winv, tally, table)
    return pl.pallas_call(
        store_kernel,
        out_shape=(
            jax.ShapeDtypeStruct((MEM, NBLK, COLS, VERT), BF16),
            jax.ShapeDtypeStruct((NBLK, MEM, MEM), BF16),
        ),
        in_specs=[vmem, vmem],
        out_specs=(hbm, hbm),
        scratch_shapes=[dma((9,))],
        compiler_params=pltpu.CompilerParams(vmem_limit_bytes=40 << 20),
        name="store",
    )(analysis, slots)


def solution(mesh):
    return jax.shard_map(
        body,
        mesh=mesh,
        in_specs=(
            P("mem", "grp", None, None),
            P("mem", "grp", None),
            P(("grp", "mem"), None),
            P(("grp", "mem"), None),
            P(("grp", "mem")),
            P(("grp", "mem")),
        ),
        out_specs=(P(None, ("grp", "mem"), None, None), P(("grp", "mem"), None, None)),
        check_vma=False,
    )
```

profile of v0, /device:TPU:1, one launch (start us, length us, event | category | flops | bytes accessed | tf_op | source)
XLA Modules:
  0.0 131.0 jit_solution(16848150931233730640)
XLA Ops:
  0.6 126.9 %analyse.1 = (bf16[128,8,8,512]{3,2,1,0:T(8,128)(2,1)S(1)}, bf16[8,128,128]{2,1,0:T(8,128)(2,1)S(1)}) custom-call(bf16[4,256,8,512]{3,2,1,0:T(8,128)(2,1)} %prior.1, bf16[4,32,8,1024]{3,2,1,0:T(8,128)(2,1)} %bitcast.1, f32[8,1024]{1,0:T(8,128)} %datum.1, bf16[8,1024]{1,0:T(8,128)(2,1)} %winv.1, s32[8]{0:T(128)} %tally.1, s32[8]{0:T(128)} %table.1), custom_call_target="tpu_custom_call" | custom-call | tf_op jit(solution)/shard_map/analyse/pallas_call | solution.py:254
  127.5 3.4 %store.1 = (bf16[128,8,8,512]{3,2,1,0:T(8,128)(2,1)}, bf16[8,128,128]{2,1,0:T(8,128)(2,1)}) custom-call(bf16[128,8,8,512]{3,2,1,0:T(8,128)(2,1)S(1)} %get-tuple-element.4.analysis, bf16[8,128,128]{2,1,0:T(8,128)(2,1)S(1)} %get-tuple-element.5.slots), custom_call_target="tpu_custom_call" | custom-call | tf_op jit(solution)/shard_map/store/pallas_call | solution.py:284
where the time goes:
time: 131 us
  Pallas kernels  130 us (99%)
    pallas_call x1, Pallas kernels, body(): pl.pallas_call(analysis_kernel, out_shape=(pltpu.VMEM((MEM, NBLK, COLS, V...  127 us
    pallas_call x1, Pallas kernels, body(): pl.pallas_call(store_kernel, out_shape=(jax.ShapeDtypeStruct((MEM, NBLK,...  3.43 us

commit v1 on v0

--- a/solution.py
+++ b/solution.py
@@ -18,6 +18,10 @@
 NMEM = 32
 OWN = MEM // NMEM
 CAP = NBLK // 2
+LAST = NBLK - 1
+HALF = OWN // 2
+PARTS = 4
+STEP = MEM // PARTS
 ROWS = MEM * COLS
 MESH = pl.DeviceIdType.MESH
 HIGH = lax.Precision.HIGHEST
@@ -30,10 +34,10 @@
 
 
 def analysis_kernel(
-    prior, equiv, datum, winv, tally, table,
-    out, slots,
-    xg, yg, yf, kron, spread, ymat, zmat, pmat, scales, wts, pack, got, tabs, tab_mine,
-    x_send, x_recv, y_send, y_recv, g_send, g_recv, t_send, t_recv, x_loc, y_loc,
+    prior, equiv, datum_hbm, winv_hbm, tally_hbm, table_hbm,
+    out, slots, xlast, klast,
+    xg, yg, datum, winv, tally, table, yf, kron, spread, ymat, zmat, pmat, scales, wts, pack, got, tabs, tab_mine,
+    x_send, x_recv, y_send, y_recv, g_send, g_recv, t_send, t_recv, x_loc, y_loc, s_loc,
 ):
     g = lax.axis_index("grp")
     m = lax.axis_index("mem")
@@ -54,33 +58,56 @@
     pl.semaphore_wait(barrier, NMEM - 1 + NGRP - 1)
 
     def send_obs(i, carry):
-        p = peer((i * 11) % NMEM)
+        p = peer((i % (NMEM - 1) + 1) * 5 % NMEM)
+        part = i // (NMEM - 1)
         pltpu.make_async_remote_copy(
-            src_ref=equiv.at[:, p], dst_ref=yg.at[pl.ds(OWN * m, OWN)],
+            src_ref=equiv.at[pl.ds(part, 1), p], dst_ref=yg.at[pl.ds(OWN * m + part, 1)],
             send_sem=y_send, recv_sem=y_recv, device_id=(g, p), device_id_type=MESH,
         ).start()
         return carry
 
-    lax.fori_loop(1, NMEM, send_obs, 0)
+    lax.fori_loop(0, OWN * (NMEM - 1), send_obs, 0)
     own_y = pltpu.make_async_copy(equiv.at[:, m], yg.at[pl.ds(OWN * m, OWN)], y_loc)
     own_y.start()
 
-    def send_block(q, carry):
+    small = [
+        pltpu.make_async_copy(a, b, s_loc.at[n])
+        for n, (a, b) in enumerate(
+            ((datum_hbm, datum), (winv_hbm, winv), (tally_hbm, tally), (table_hbm, table)))
+    ]
+    for c in small:
+        c.start()
+
+    def send_block(q, land, sem):
         def send_prior(i, inner):
-            p = peer((i * 11) % NMEM)
+            p = peer((i % (NMEM - 1) + 1) * 5 % NMEM)
+            part = HALF * (i // (NMEM - 1))
             pltpu.make_async_remote_copy(
-                src_ref=prior.at[:, pl.ds(NBLK * p + q, 1)],
-                dst_ref=xg.at[pl.ds(OWN * m, OWN), pl.ds(q, 1)],
-                send_sem=x_send, recv_sem=x_recv.at[q], device_id=(g, p), device_id_type=MESH,
+                src_ref=prior.at[pl.ds(part, HALF), pl.ds(NBLK * p + q, 1)],
+                dst_ref=land(pl.ds(OWN * m + part, HALF)),
+                send_sem=sem, recv_sem=x_recv.at[q], device_id=(g, p), device_id_type=MESH,
             ).start()
             return inner
 
-        return lax.fori_loop(1, NMEM, send_prior, carry)
-
-    lax.fori_loop(0, NBLK, send_block, 0)
-    own_x = pltpu.make_async_copy(
-        prior.at[:, pl.ds(NBLK * m, NBLK)], xg.at[pl.ds(OWN * m, OWN)], x_loc)
-    own_x.start()
+        return lax.fori_loop(0, OWN // HALF * (NMEM - 1), send_prior, 0)
+
+    def send_early(q, carry):
+        send_block(q, lambda rows: xg.at[rows, pl.ds(q, 1)], x_send.at[0])
+        return carry
+
+    lax.fori_loop(0, LAST, send_early, 0)
+    send_block(LAST, lambda rows: xlast.at[rows], x_send.at[1])
+    own_x = [
+        pltpu.make_async_copy(
+            prior.at[:, pl.ds(NBLK * m, LAST)], xg.at[pl.ds(OWN * m, OWN)], x_loc.at[0]),
+        pltpu.make_async_copy(
+            prior.at[:, pl.ds(NBLK * m + LAST, 1)], xlast.at[pl.ds(OWN * m, OWN)], x_loc.at[1]),
+    ]
+    for c in own_x:
+        c.start()
+
+    for c in small:
+        c.wait()
 
     for j in range(NBLK):
         tab_mine[j:j + 1, :] = jnp.full((1, 128), table[j], jnp.int32)
@@ -181,13 +208,17 @@
         == lax.broadcasted_iota(jnp.int32, (COLS, ROWS), 1) % COLS
     ).astype(F32)
 
-    def expand(b, carry):
+    def expanded(b):
         wide = lax.dot_general(
             wts[b], spread[...], (((0,), (0,)), ((), ())), preferred_element_type=F32)
-        kron[b] = (wide[:, None, :] * mask[None]).reshape(ROWS, ROWS).astype(BF16)
-        return carry
-
-    lax.fori_loop(0, NBLK, expand, 0)
+        return (wide[:, None, :] * mask[None]).reshape(ROWS, ROWS).astype(BF16)
+
+    def expand(b, carry):
+        kron[b] = expanded(b)
+        return carry
+
+    lax.fori_loop(0, LAST, expand, 0)
+    klast[...] = expanded(LAST)
 
     for c in tab_copies:
         c.wait()
@@ -210,60 +241,77 @@
                 acc = jnp.where(ranks[gg * CAP + w] == k, got[gg, w].astype(F32), acc)
         slots[k] = acc.astype(BF16)
 
-    own_x.wait()
-    step = MEM // 4
+    for c in own_x:
+        c.wait()
 
     def mix(q, carry):
         here = xg.at[pl.ds(0, MEM - OWN), pl.ds(q, 1)]
         pltpu.make_async_copy(here, here, x_recv.at[q]).wait()
         state = xg[:, q].astype(F32).reshape(ROWS, VERT).astype(BF16)
-        for part in range(4):
-            mixed = jnp.dot(
-                kron[q, part * step * COLS:(part + 1) * step * COLS, :], state,
-                preferred_element_type=F32)
-            out[part * step:(part + 1) * step, q] = mixed.reshape(step, COLS, VERT).astype(BF16)
-        return carry
-
-    lax.fori_loop(0, NBLK, mix, 0)
+        for part in range(PARTS):
+            out[part * STEP:(part + 1) * STEP, q] = mixed(kron.at[q], state, part)
+        return carry
+
+    lax.fori_loop(0, LAST, mix, 0)
+    here = xlast.at[pl.ds(0, MEM - OWN)]
+    pltpu.make_async_copy(here, here, x_recv.at[LAST]).wait()
 
     sent = yg.at[pl.ds(0, MEM - OWN)]
     pltpu.make_async_copy(sent, sent, y_send).wait()
     sent = xg.at[pl.ds(0, MEM - OWN)]
-    pltpu.make_async_copy(sent, sent, x_send).wait()
-
-
-def store_kernel(analysis, slots, out, out_slots, sems):
-    part = MEM // 8
+    pltpu.make_async_copy(sent, sent, x_send.at[0]).wait()
+    sent = xlast.at[pl.ds(0, MEM - OWN)]
+    pltpu.make_async_copy(sent, sent, x_send.at[1]).wait()
+
+
+def mixed(weights, state, part):
+    rows = weights[part * STEP * COLS:(part + 1) * STEP * COLS, :]
+    total = jnp.dot(rows, state, preferred_element_type=F32)
+    return total.reshape(STEP, COLS, VERT).astype(BF16)
+
+
+def store_kernel(analysis, slots, xlast, klast, out, out_slots, made, sems):
     copies = [
-        pltpu.make_async_copy(analysis.at[pl.ds(k * part, part)], out.at[pl.ds(k * part, part)], sems.at[k])
-        for k in range(8)
+        pltpu.make_async_copy(analysis, out.at[:, pl.ds(0, LAST)], sems.at[PARTS]),
+        pltpu.make_async_copy(slots, out_slots, sems.at[PARTS + 1]),
     ]
-    copies.append(pltpu.make_async_copy(slots, out_slots, sems.at[8]))
     for c in copies:
         c.start()
+    state = xlast[:, 0].astype(F32).reshape(ROWS, VERT).astype(BF16)
+    for part in range(PARTS):
+        rows = pl.ds(part * STEP, STEP)
+        made[rows, 0] = mixed(klast, state, part)
+        c = pltpu.make_async_copy(made.at[rows], out.at[rows, pl.ds(LAST, 1)], sems.at[part])
+        c.start()
+        copies.append(c)
     for c in copies:
         c.wait()
 
 
 def body(prior, equiv, datum, winv, tally, table):
     vmem = pl.BlockSpec(memory_space=pltpu.VMEM)
-    smem = pl.BlockSpec(memory_space=pltpu.SMEM)
     hbm = pl.BlockSpec(memory_space=pltpu.HBM)
     dma = pltpu.SemaphoreType.DMA
     equiv = equiv.reshape(OWN, NMEM, NBLK, OBS)
-    analysis, slots = pl.pallas_call(
+    made = pl.pallas_call(
         analysis_kernel,
         out_shape=(
-            pltpu.VMEM((MEM, NBLK, COLS, VERT), BF16),
+            pltpu.VMEM((MEM, LAST, COLS, VERT), BF16),
             pltpu.VMEM((NBLK, MEM, MEM), BF16),
+            pltpu.VMEM((MEM, 1, COLS, VERT), BF16),
+            pltpu.VMEM((ROWS, ROWS), BF16),
         ),
-        in_specs=[hbm, hbm, vmem, vmem, smem, smem],
-        out_specs=(vmem, vmem),
+        in_specs=[hbm] * 6,
+        out_specs=(vmem,) * 4,
         scratch_shapes=[
-            pltpu.VMEM((MEM, NBLK, COLS, VERT), BF16),
+            pltpu.VMEM((MEM, LAST, COLS, VERT), BF16),
             pltpu.VMEM((MEM, NBLK, OBS), BF16),
+            pltpu.VMEM((NBLK, OBS), F32),
+            pltpu.VMEM((NBLK, OBS), BF16),
+            pltpu.SMEM((NBLK,), jnp.int32),
+            pltpu.SMEM((NBLK,), jnp.int32),
             pltpu.VMEM((OBS // 128, MEM * NBLK, 128), F32),
-            pltpu.VMEM((NBLK, ROWS, ROWS), BF16),
+            pltpu.VMEM((LAST, ROWS, ROWS), BF16),
             pltpu.VMEM((MEM, ROWS), BF16),
             pltpu.VMEM((NBLK, MEM, MEM), F32),
             pltpu.VMEM((NBLK, MEM, MEM), F32),
@@ -274,11 +322,11 @@
             pltpu.VMEM((NGRP, CAP, MEM, MEM), BF16),
             pltpu.VMEM((NGRP, NBLK, 128), jnp.int32),
             pltpu.VMEM((NBLK, 128), jnp.int32),
-            dma, dma((NBLK,)), dma, dma,
-            dma((NGRP,)), dma((NGRP,)), dma((NGRP,)), dma((NGRP,)), dma, dma,
+            dma((2,)), dma((NBLK,)), dma, dma,
+            dma((NGRP,)), dma((NGRP,)), dma((NGRP,)), dma((NGRP,)), dma((2,)), dma, dma((4,)),
         ],
         compiler_params=pltpu.CompilerParams(
-            collective_id=0, has_side_effects=True, vmem_limit_bytes=50 << 20),
+            collective_id=0, has_side_effects=True, vmem_limit_bytes=46 << 20),
         name="analyse",
     )(prior, equiv, datum, winv, tally, table)
     return pl.pallas_call(
@@ -287,12 +335,12 @@
             jax.ShapeDtypeStruct((MEM, NBLK, COLS, VERT), BF16),
             jax.ShapeDtypeStruct((NBLK, MEM, MEM), BF16),
         ),
-        in_specs=[vmem, vmem],
+        in_specs=[vmem] * 4,
         out_specs=(hbm, hbm),
-        scratch_shapes=[dma((9,))],
+        scratch_shapes=[pltpu.VMEM((MEM, 1, COLS, VERT), BF16), dma((PARTS + 2,))],
         compiler_params=pltpu.CompilerParams(vmem_limit_bytes=40 << 20),
         name="store",
-    )(analysis, slots)
+    )(*made)
 
 
 def solution(mesh):

time: 131 us -> 129 us (0.985)
  Pallas kernels: 130 us -> 128 us
    pallas_call x1, Pallas kernels: 127 us -> 124 us  [body(): pl.pallas_call(analysis_kernel, out_shape=(pltpu.VMEM((MEM, LAST, COLS, V...]
where the time goes in v1:
time: 129 us
  Pallas kernels  128 us (99%)
    pallas_call x1, Pallas kernels, body(): pl.pallas_call(analysis_kernel, out_shape=(pltpu.VMEM((MEM, LAST, COLS, V...  124 us
    pallas_call x1, Pallas kernels, body(): pl.pallas_call(store_kernel, out_shape=(jax.ShapeDtypeStruct((MEM, NBLK,...  3.5 us

profile of v1, /device:TPU:1, one launch (start us, length us, event | category | flops | bytes accessed | tf_op | source)
XLA Modules:
  0.0 128.5 jit_solution(16902840615668707286)
XLA Ops:
  0.6 124.4 %analyse.1 = (bf16[128,7,8,512]{3,2,1,0:T(8,128)(2,1)S(1)}, bf16[8,128,128]{2,1,0:T(8,128)(2,1)S(1)}, bf16[128,1,8,512]{3,2,1,0:T(8,128)(2,1)S(1)}, bf16[1024,1024]{1,0:T(8,128)(2,1)S(1)}) custom-call(bf16[4,256,8,512]{3,2,1,0:T(8,128)(2,1)} %prior.1, bf16[4,32,8,1024]{3,2,1,0:T(8,128)(2,1)} %bitcast.1, f32[8,1024]{1,0:T(8,128)} %datum_hbm.1, ...), custom_call_target="tpu_custom_call" | custom-call | tf_op jit(solution)/shard_map/analyse/pallas_call | solution.py:296
  125.0 3.5 %store.1 = (bf16[128,8,8,512]{3,2,1,0:T(8,128)(2,1)}, bf16[8,128,128]{2,1,0:T(8,128)(2,1)}) custom-call(bf16[128,7,8,512]{3,2,1,0:T(8,128)(2,1)S(1)} %get-tuple-element.6.analysis, bf16[8,128,128]{2,1,0:T(8,128)(2,1)S(1)} %get-tuple-element.7.slots, bf16[128,1,8,512]{3,2,1,0:T(8,128)(2,1)S(1)} %get-tuple-element.8.xlast, ...), custom_call_target="tpu_custom_call" | custom-call | tf_op jit(solution)/shard_map/store/pallas_call | solution.py:332

commit v2 on v1

--- a/solution.py
+++ b/solution.py
@@ -96,7 +96,15 @@
         return carry
 
     lax.fori_loop(0, LAST, send_early, 0)
-    send_block(LAST, lambda rows: xlast.at[rows], x_send.at[1])
+    far = sorted(range(1, NMEM), key=lambda i: -(min(i // 8, 4 - i // 8) + min((i // 2) % 4, 4 - (i // 2) % 4)))
+    for i in far:
+        for part in range(0, OWN, HALF):
+            p = peer(i)
+            pltpu.make_async_remote_copy(
+                src_ref=prior.at[pl.ds(part, HALF), pl.ds(NBLK * p + LAST, 1)],
+                dst_ref=xlast.at[pl.ds(OWN * m + part, HALF)],
+                send_sem=x_send.at[1], recv_sem=x_recv.at[LAST], device_id=(g, p), device_id_type=MESH,
+            ).start()
     own_x = [
         pltpu.make_async_copy(
             prior.at[:, pl.ds(NBLK * m, LAST)], xg.at[pl.ds(OWN * m, OWN)], x_loc.at[0]),

time: 129 us -> 127 us (0.984)
  no operation moved by 1% of the time
where the time goes in v2:
time: 127 us
  Pallas kernels  127 us (100%)
    pallas_call x1, Pallas kernels, body(): pl.pallas_call(analysis_kernel, out_shape=(pltpu.VMEM((MEM, LAST, COLS, V...  123 us
    pallas_call x1, Pallas kernels, body(): pl.pallas_call(store_kernel, out_shape=(jax.ShapeDtypeStruct((MEM, NBLK,...  3.5 us

profile of v2, /device:TPU:1, one launch (start us, length us, event | category | flops | bytes accessed | tf_op | source)
XLA Modules:
  0.0 127.3 jit_solution(10729263487374415212)
XLA Ops:
  0.6 123.1 %analyse.1 = (bf16[128,7,8,512]{3,2,1,0:T(8,128)(2,1)S(1)}, bf16[8,128,128]{2,1,0:T(8,128)(2,1)S(1)}, bf16[128,1,8,512]{3,2,1,0:T(8,128)(2,1)S(1)}, bf16[1024,1024]{1,0:T(8,128)(2,1)S(1)}) custom-call(bf16[4,256,8,512]{3,2,1,0:T(8,128)(2,1)} %prior.1, bf16[4,32,8,1024]{3,2,1,0:T(8,128)(2,1)} %bitcast.1, f32[8,1024]{1,0:T(8,128)} %datum_hbm.1, ...), custom_call_target="tpu_custom_call" | custom-call | tf_op jit(solution)/shard_map/analyse/pallas_call | solution.py:304
  123.8 3.5 %store.1 = (bf16[128,8,8,512]{3,2,1,0:T(8,128)(2,1)}, bf16[8,128,128]{2,1,0:T(8,128)(2,1)}) custom-call(bf16[128,7,8,512]{3,2,1,0:T(8,128)(2,1)S(1)} %get-tuple-element.6.analysis, bf16[8,128,128]{2,1,0:T(8,128)(2,1)S(1)} %get-tuple-element.7.slots, bf16[128,1,8,512]{3,2,1,0:T(8,128)(2,1)S(1)} %get-tuple-element.8.xlast, ...), custom_call_target="tpu_custom_call" | custom-call | tf_op jit(solution)/shard_map/store/pallas_call | solution.py:340

commit v3 on v2

--- a/solution.py
+++ b/solution.py
@@ -46,13 +46,15 @@
     def peer(i):
         return (((row + i // 8) % 4) * 4 + (col + (i // 2) % 4) % 4) * 2 + (core + i % 2) % 2
 
+    rows = [lax.rem(row + d, 4) * 8 for d in range(4)]
+    cols = [lax.rem(col + d, 4) * 2 for d in range(4)]
+    cores = [core, 1 - core]
+    peers = [rows[i // 8] + cols[(i // 2) % 4] + cores[i % 2] for i in range(NMEM)]
+
     barrier = pltpu.get_barrier_semaphore()
 
-    def greet(i, carry):
-        pl.semaphore_signal(barrier, inc=1, device_id=(g, peer(i)), device_id_type=MESH)
-        return carry
-
-    lax.fori_loop(1, NMEM, greet, 0)
+    for i in range(1, NMEM):
+        pl.semaphore_signal(barrier, inc=1, device_id=(g, peers[i]), device_id_type=MESH)
     for d in range(1, NGRP):
         pl.semaphore_signal(barrier, inc=1, device_id=((g + d) % NGRP, m), device_id_type=MESH)
     pl.semaphore_wait(barrier, NMEM - 1 + NGRP - 1)
@@ -99,7 +101,7 @@
     far = sorted(range(1, NMEM), key=lambda i: -(min(i // 8, 4 - i // 8) + min((i // 2) % 4, 4 - (i // 2) % 4)))
     for i in far:
         for part in range(0, OWN, HALF):
-            p = peer(i)
+            p = peers[i]
             pltpu.make_async_remote_copy(
                 src_ref=prior.at[pl.ds(part, HALF), pl.ds(NBLK * p + LAST, 1)],
                 dst_ref=xlast.at[pl.ds(OWN * m + part, HALF)],

time: 127 us -> 127 us (level)
  no operation moved by 1% of the time
where the time goes in v3:
time: 127 us
  Pallas kernels  126 us (99%)
    pallas_call x1, Pallas kernels, body(): pl.pallas_call(analysis_kernel, out_shape=(pltpu.VMEM((MEM, LAST, COLS, V...  123 us
    pallas_call x1, Pallas kernels, body(): pl.pallas_call(store_kernel, out_shape=(jax.ShapeDtypeStruct((MEM, NBLK,...  3.5 us

profile of v3, /device:TPU:1, one launch (start us, length us, event | category | flops | bytes accessed | tf_op | source)
XLA Modules:
  0.0 126.9 jit_solution(9121886829479838449)
XLA Ops:
  0.6 122.7 %analyse.1 = (bf16[128,7,8,512]{3,2,1,0:T(8,128)(2,1)S(1)}, bf16[8,128,128]{2,1,0:T(8,128)(2,1)S(1)}, bf16[128,1,8,512]{3,2,1,0:T(8,128)(2,1)S(1)}, bf16[1024,1024]{1,0:T(8,128)(2,1)S(1)}) custom-call(bf16[4,256,8,512]{3,2,1,0:T(8,128)(2,1)} %prior.1, bf16[4,32,8,1024]{3,2,1,0:T(8,128)(2,1)} %bitcast.1, f32[8,1024]{1,0:T(8,128)} %datum_hbm.1, ...), custom_call_target="tpu_custom_call" | custom-call | tf_op jit(solution)/shard_map/analyse/pallas_call | solution.py:306
  123.3 3.5 %store.1 = (bf16[128,8,8,512]{3,2,1,0:T(8,128)(2,1)}, bf16[8,128,128]{2,1,0:T(8,128)(2,1)}) custom-call(bf16[128,7,8,512]{3,2,1,0:T(8,128)(2,1)S(1)} %get-tuple-element.6.analysis, bf16[8,128,128]{2,1,0:T(8,128)(2,1)S(1)} %get-tuple-element.7.slots, bf16[128,1,8,512]{3,2,1,0:T(8,128)(2,1)S(1)} %get-tuple-element.8.xlast, ...), custom_call_target="tpu_custom_call" | custom-call | tf_op jit(solution)/shard_map/store/pallas_call | solution.py:342

commit v4 on v3

--- a/solution.py
+++ b/solution.py
@@ -51,9 +51,11 @@
     cores = [core, 1 - core]
     peers = [rows[i // 8] + cols[(i // 2) % 4] + cores[i % 2] for i in range(NMEM)]
 
+    far = sorted(range(1, NMEM), key=lambda i: -(min(i // 8, 4 - i // 8) + min((i // 2) % 4, 4 - (i // 2) % 4)))
+
     barrier = pltpu.get_barrier_semaphore()
 
-    for i in range(1, NMEM):
+    for i in far:
         pl.semaphore_signal(barrier, inc=1, device_id=(g, peers[i]), device_id_type=MESH)
     for d in range(1, NGRP):
         pl.semaphore_signal(barrier, inc=1, device_id=((g + d) % NGRP, m), device_id_type=MESH)
@@ -98,8 +100,7 @@
         return carry
 
     lax.fori_loop(0, LAST, send_early, 0)
-    far = sorted(range(1, NMEM), key=lambda i: -(min(i // 8, 4 - i // 8) + min((i // 2) % 4, 4 - (i // 2) % 4)))
-    for i in far:
+    for i in far[-1:] + far[:-1]:
         for part in range(0, OWN, HALF):
             p = peers[i]
             pltpu.make_async_remote_copy(

time: 127 us -> 127 us (level)
  no operation moved by 1% of the time
where the time goes in v4:
time: 127 us
  Pallas kernels  126 us (99%)
    pallas_call x1, Pallas kernels, body(): pl.pallas_call(analysis_kernel, out_shape=(pltpu.VMEM((MEM, LAST, COLS, V...  123 us
    pallas_call x1, Pallas kernels, body(): pl.pallas_call(store_kernel, out_shape=(jax.ShapeDtypeStruct((MEM, NBLK,...  3.5 us

profile of v4, /device:TPU:1, one launch (start us, length us, event | category | flops | bytes accessed | tf_op | source)
XLA Modules:
  0.0 126.8 jit_solution(8546237724839375692)
XLA Ops:
  0.6 122.7 %analyse.1 = (bf16[128,7,8,512]{3,2,1,0:T(8,128)(2,1)S(1)}, bf16[8,128,128]{2,1,0:T(8,128)(2,1)S(1)}, bf16[128,1,8,512]{3,2,1,0:T(8,128)(2,1)S(1)}, bf16[1024,1024]{1,0:T(8,128)(2,1)S(1)}) custom-call(bf16[4,256,8,512]{3,2,1,0:T(8,128)(2,1)} %prior.1, bf16[4,32,8,1024]{3,2,1,0:T(8,128)(2,1)} %bitcast.1, f32[8,1024]{1,0:T(8,128)} %datum_hbm.1, ...), custom_call_target="tpu_custom_call" | custom-call | tf_op jit(solution)/shard_map/analyse/pallas_call | solution.py:307
  123.3 3.5 %store.1 = (bf16[128,8,8,512]{3,2,1,0:T(8,128)(2,1)}, bf16[8,128,128]{2,1,0:T(8,128)(2,1)}) custom-call(bf16[128,7,8,512]{3,2,1,0:T(8,128)(2,1)S(1)} %get-tuple-element.6.analysis, bf16[8,128,128]{2,1,0:T(8,128)(2,1)S(1)} %get-tuple-element.7.slots, bf16[128,1,8,512]{3,2,1,0:T(8,128)(2,1)S(1)} %get-tuple-element.8.xlast, ...), custom_call_target="tpu_custom_call" | custom-call | tf_op jit(solution)/shard_map/store/pallas_call | solution.py:343
